TPU v7x, 32 devices: a whole 2x2x4 slice. The times are simulated.
32 devices in a mesh: group: 8 (over z, x), local: 4 (over y, core).
Axes of the slice: x: 2, y: 2, z: 4, core: 2. Of those that a mesh axis runs over, the one named last changes fastest.
Arguments:
- states_in: bfloat16 [32, 7168], P(('group', 'local')), may hold values from -24 to 24
- queries: bfloat16 [32, 128, 576], P(('group', 'local')), may hold values from -320 to 320
- kv_cache: bfloat16 [32, 1024, 576], P(('group', 'local')), may hold values from -5 to 5
- kv_new: bfloat16 [32, 576], P(('group', 'local')), may hold values from -12 to 12
- lengths: int32 [32], P(('group', 'local')), may hold values from 2 to 1024, as said below
- w_uv: bfloat16 [128, 512, 128], P(('group', 'local')), may hold values from -1.5 to 1.5
- w_out: bfloat16 [16384, 7168], P(('group', 'local')), may hold values from -0.046875 to 0.046875
- norm_gain: float32 [7168], replicated, may hold values from 0.25 to 1.75
- expert_ids: int32 [32, 8], P(('group', 'local')), may hold values from 0 to 23, as said below
- route_scores: float32 [32, 8], P(('group', 'local')), may hold values from 0.05 to 1
- w_gate: bfloat16 [24, 7168, 1024], P('group', None, 'local'), may hold values from -0.0625 to 0.0625
- w_up: bfloat16 [24, 7168, 1024], P('group', None, 'local'), may hold values from -0.0625 to 0.0625
- w_down: bfloat16 [24, 1024, 7168], P('group', 'local'), may hold values from -0.1875 to 0.1875
Outputs:
- residual: bfloat16 [32, 7168], P(('group', 'local'))
- layer_out: bfloat16 [32, 7168], P(('group', 'local'))
Inputs may be any that keep to these rules, and one draw needn't show every extreme that they name: Each request attends to the first lengths entries of its cache and to its new token; some request has all 1024. `expert_ids`: each row names 8 different experts, all within at most 4 groups, where group g holds experts g * 3 to g * 3 + 2.
All inputs are finite; a program needn't handle non-finite values.
Results may differ from a plain program's by a relative error of at most 0.015.
Values may be sent and summed in bfloat16 or wider, within the bound.
A program may use at most 128 MiB of HBM per device.

v0:
```python
import jax
import jax.numpy as jnp
from jax import lax
from jax.sharding import PartitionSpec as P

LAT = 512
ROPE = 64
VD = 128
NGRP = 8


def expert_term(slot_rows, weights, w_gate, w_up, w_down):
    result = jnp.zeros((slot_rows.shape[0], w_down.shape[2]), jnp.float32)
    for expert in range(w_gate.shape[0]):
        gate_proj = jnp.dot(slot_rows, w_gate[expert], preferred_element_type=jnp.float32)
        up_proj = jnp.dot(slot_rows, w_up[expert], preferred_element_type=jnp.float32)
        active = (jax.nn.silu(gate_proj) * up_proj).astype(jnp.bfloat16)
        output = jnp.dot(active, w_down[expert], preferred_element_type=jnp.float32)
        result = result + weights[:, expert : expert + 1].astype(jnp.float32) * output
    return result


def body(
    states_in,
    queries,
    kv_cache,
    kv_new,
    lengths,
    w_uv,
    w_out,
    norm_gain,
    expert_ids,
    route_scores,
    w_gate,
    w_up,
    w_down,
):
    requests = queries.shape[0]
    cache_len = kv_cache.shape[1]
    group_count = lax.axis_size("group")
    local_count = lax.axis_size("local")
    softmax_scale = (VD + ROPE) ** (-0.5)
    cached = (
        jnp.einsum("rhc,rkc->rhk", queries, kv_cache, preferred_element_type=jnp.float32)
        * softmax_scale
    )
    own_score = (
        jnp.einsum("rhc,rc->rh", queries, kv_new, preferred_element_type=jnp.float32)
        * softmax_scale
    )
    visible = lax.broadcasted_iota(jnp.int32, (requests, 1, cache_len), 2) < lengths[:, None, None]
    highest = jnp.maximum(jnp.max(jnp.where(visible, cached, -1e30), axis=2), own_score)
    weights_cached = jnp.exp(jnp.where(visible, cached - highest[:, :, None], -1e30))
    weight_own = jnp.exp(own_score - highest)
    denominator = jnp.sum(weights_cached, axis=2) + weight_own
    probs_cached = (weights_cached / denominator[:, :, None]).astype(jnp.bfloat16)
    prob_own = (weight_own / denominator).astype(jnp.bfloat16)
    blended = jnp.einsum(
        "rhk,rkl->rhl", probs_cached, kv_cache[:, :, :LAT], preferred_element_type=jnp.float32
    )
    blended = blended + prob_own.astype(jnp.float32)[:, :, None] * kv_new[:, None, :LAT].astype(
        jnp.float32
    )
    latent_out = blended.astype(jnp.bfloat16)
    by_head = lax.all_to_all(
        latent_out, ("group", "local"), split_axis=1, concat_axis=0, tiled=True
    )
    rows_total = by_head.shape[0]
    head_values = jnp.einsum(
        "rhl,hlv->rhv", by_head, w_uv, preferred_element_type=jnp.float32
    ).astype(jnp.bfloat16)
    value_rows = head_values.reshape(rows_total, -1)
    attention = lax.psum_scatter(
        jnp.dot(value_rows, w_out, preferred_element_type=jnp.float32),
        ("group", "local"),
        scatter_dimension=0,
        tiled=True,
    )
    residual = (states_in.astype(jnp.float32) + attention).astype(jnp.bfloat16)
    widened = residual.astype(jnp.float32)
    normed = (
        widened * lax.rsqrt(jnp.mean(widened * widened, axis=1, keepdims=True) + 1e-06) * norm_gain
    ).astype(jnp.bfloat16)
    route_weights = (2.5 * route_scores / jnp.sum(route_scores, axis=1, keepdims=True)).astype(
        jnp.bfloat16
    )
    per_block = w_gate.shape[0]
    expert_total = per_block * group_count
    span = group_count // NGRP
    experts_in_group = per_block * span
    chosen = expert_ids[:, :, None] == lax.broadcasted_iota(jnp.int32, (1, 1, expert_total), 2)
    dense_weights = jnp.sum(
        jnp.where(chosen, route_weights.astype(jnp.float32)[:, :, None], 0.0), axis=1
    )
    by_block = dense_weights.reshape(requests, group_count, per_block)
    block_group = lax.broadcasted_iota(jnp.int32, (1, 1, group_count), 2) // span
    in_group = jnp.any(expert_ids[:, :, None] // experts_in_group == block_group, axis=1)
    position = jnp.cumsum(in_group.astype(jnp.int32), axis=0) - 1
    slot_index = lax.broadcasted_iota(jnp.int32, (group_count, requests, requests), 1)
    packing = in_group.T[:, None, :] & (position.T[:, None, :] == slot_index)
    pack_half = packing.astype(jnp.bfloat16)
    send_rows = jnp.einsum(
        "gcr,rd->gcd", pack_half, normed, preferred_element_type=jnp.float32
    ).astype(jnp.bfloat16)
    send_weights = jnp.einsum(
        "gcr,rgj->gcj", packing.astype(jnp.float32), by_block, precision=lax.Precision.HIGHEST
    ).astype(jnp.bfloat16)
    copies = jnp.broadcast_to(
        send_rows[:, None], (group_count, local_count) + send_rows.shape[1:]
    ).reshape(group_count * local_count, requests, send_rows.shape[2])
    copies_weights = jnp.broadcast_to(
        send_weights[:, None], (group_count, local_count) + send_weights.shape[1:]
    ).reshape(group_count * local_count, requests, send_weights.shape[2])
    got_rows, got_weights = (
        lax.all_to_all(copies, ("group", "local"), split_axis=0, concat_axis=0, tiled=True),
        lax.all_to_all(copies_weights, ("group", "local"), split_axis=0, concat_axis=0, tiled=True),
    )
    partial_sums = expert_term(
        got_rows.reshape(-1, got_rows.shape[2]),
        got_weights.reshape(-1, got_weights.shape[2]),
        w_gate,
        w_up,
        w_down,
    )
    came_back = lax.all_to_all(
        partial_sums.reshape(group_count * local_count, requests, partial_sums.shape[1]).astype(
            jnp.bfloat16
        ),
        ("group", "local"),
        split_axis=0,
        concat_axis=0,
        tiled=True,
    ).astype(jnp.float32)
    returned = jnp.sum(
        came_back.reshape(group_count, local_count, requests, came_back.shape[2]), axis=1
    ).astype(jnp.bfloat16)
    expert_sum = jnp.einsum("gcr,gcd->rd", pack_half, returned, preferred_element_type=jnp.float32)
    layer_out = (residual.astype(jnp.float32) + expert_sum).astype(jnp.bfloat16)
    return (residual, layer_out)


def solution(mesh):
    in_specs = (
        P(("group", "local"), None),
        P(("group", "local"), None, None),
        P(("group", "local"), None, None),
        P(("group", "local"), None),
        P(("group", "local")),
        P(("group", "local"), None, None),
        P(("group", "local"), None),
        P(),
        P(("group", "local"), None),
        P(("group", "local"), None),
        P("group", None, "local"),
        P("group", None, "local"),
        P("group", "local", None),
    )
    out_specs = (P(("group", "local"), None), P(("group", "local"), None))
    return jax.shard_map(body, mesh=mesh, in_specs=in_specs, out_specs=out_specs, check_vma=False)
```

profile of v0, /device:TPU:0, one launch (start us, length us, event | category | flops | bytes accessed | tf_op | source)
XLA Modules:
  0.0 245.3 jit_solution(12620266545381693669)
XLA Ops:
  7.9 0.7 slice_convert_fusion
  8.6 1.8 select_reduce_fusion
  10.4 1.1 fusion.109
  11.5 0.2 fusion.69
  11.8 1.7 fusion.31
  13.5 0.2 copy.53
  13.7 0.5 broadcast.224
  14.2 1.3 reduce.13
  15.6 0.7 reshape.365
  16.3 7.3 %all-to-all-start = ((bf16[32,2,1024]{2,1,0:T(2,128)(2,1)}), bf16[32,2,1024]{2,1,0:T(2,128)(2,1)S(1)}, u32[]{:S(2)}, u32[]{:S(2)}) async-start(bf16[32,2,1024]{2,1,0:T(2,128)(2,1)} %reshape.365), calls=%async_computation | async-start | bytes 262144 | tf_op jit(solution)/shard_map/all_to_all | solution.py:65
  23.7 0.6 reduce_sum.46
  24.3 0.6 bitcast_convert_fusion.3
  24.9 0.1 select_reduce_fusion.1
  25.1 6.8 %all-to-all-done = bf16[32,2,1024]{2,1,0:T(2,128)(2,1)S(1)} async-done(((bf16[32,2,1024]{2,1,0:T(2,128)(2,1)}), bf16[32,2,1024]{2,1,0:T(2,128)(2,1)S(1)}, u32[]{:S(2)}, u32[]{:S(2)}) %all-to-all-start) | async-done | bytes 131104 | tf_op jit(solution)/shard_map/all_to_all | solution.py:65
  31.8 0.1 reshape.366
  31.9 0.7 bitcast_reduce_fusion
  32.7 0.2 fusion.32
  32.9 5.5 %fusion.77 = f32[32,7168]{1,0:T(8,128)} fusion(bf16[512,7168]{1,0:T(8,128)(2,1)} %param.19, bf16[4,4,8,128]{3,2,1,0:T(8,128)(2,1)S(1)} %fusion.32), kind=kOutput, calls=%fused_computation.68 | convolution fusion | flops 234881024 | bytes 8290304 | tf_op jit(solution)/shard_map/dot_general | solution.py:74
  38.4 0.1 fusion.99
  38.7 0.1 copy.37
  38.8 0.1 broadcast_in_dim.65
  38.9 0.7 copy.38
  39.7 2.5 %all-to-all-start.1 = ((bf16[32,1,3]{2,1,0:T(2,128)(2,1)}), bf16[32,1,3]{2,1,0:T(2,128)(2,1)S(1)}, u32[]{:S(2)}, u32[]{:S(2)}) async-start(bf16[32,1,3]{2,1,0:T(2,128)(2,1)} %copy.38), calls=%async_computation.1 | async-start | bytes 32768 | tf_op jit(solution)/shard_map/all_to_all | solution.py:116
  42.2 123.1 %all-reduce.3.cloned.1.call-done = f32[32,7168]{1,0:T(8,128)} async-done(((f32[32,7168]{1,0:T(8,128)}), f32[32,7168]{1,0:T(8,128)}) %all-reduce.3.cloned.1.call-update) | async-done | bytes 917520
  165.3 1.6 multiply_reduce_fusion
  167.7 0.1 broadcast_in_dim.67
  167.9 0.4 broadcast_in_dim.69
  168.3 3.4 %reduce.14 = bf16[32,7168]{1,0:T(8,128)(2,1)S(1)} reduce(bf16[32,1,7168]{2,1,0:T(2,128)(2,1)S(1)} %broadcast_in_dim.69, bf16[]{:T(256)} %broadcast.224), dimensions={1}, to_apply=%broadcast_in_dim.69.reduce_sub_computation | reduce | bytes 917506 | tf_op jit(solution)/shard_map/broadcast_in_dim | solution.py:108
  171.7 1.1 reshape.367
  172.8 3.7 %all-to-all-start.2 = ((bf16[32,2,3584]{2,1,0:T(2,128)(2,1)}), bf16[32,2,3584]{2,1,0:T(2,128)(2,1)S(1)}, u32[]{:S(2)}, u32[]{:S(2)}) async-start(bf16[32,2,3584]{2,1,0:T(2,128)(2,1)} %reshape.367), calls=%async_computation.2 | async-start | bytes 917504 | tf_op jit(solution)/shard_map/all_to_all | solution.py:115
  176.6 0.1 copy.39
  176.7 14.1 %all-to-all-done.2 = bf16[32,2,3584]{2,1,0:T(2,128)(2,1)S(1)} async-done(((bf16[32,2,3584]{2,1,0:T(2,128)(2,1)}), bf16[32,2,3584]{2,1,0:T(2,128)(2,1)S(1)}, u32[]{:S(2)}, u32[]{:S(2)}) %all-to-all-start.2) | async-done | bytes 458784 | tf_op jit(solution)/shard_map/all_to_all | solution.py:115
  190.7 0.4 reshape.368
  191.1 0.2 copy.43
  191.3 2.8 %fusion.13 = f32[32,256]{1,0:T(8,128)S(1)} fusion(bf16[3,7168,256]{2,1,0:T(8,128)(2,1)} %param.23, bf16[32,1,7168]{2,0,1:T(8,128)(2,1)S(1)} %copy.43), kind=kOutput, calls=%fused_computation.17 | convolution fusion | flops 117440512 | bytes 4161536 | tf_op jit(solution)/shard_map/dot_general | solution.py:15
  194.0 2.8 %fusion.8 = f32[32,256]{1,0:T(8,128)S(1)} fusion(bf16[3,7168,256]{2,1,0:T(8,128)(2,1)} %param.23, bf16[32,1,7168]{2,0,1:T(8,128)(2,1)S(1)} %copy.43), kind=kOutput, calls=%fused_computation.12 | convolution fusion | flops 117440512 | bytes 4161536 | tf_op jit(solution)/shard_map/dot_general | solution.py:15
  196.8 2.8 %fusion.18 = f32[32,256]{1,0:T(8,128)S(1)} fusion(bf16[3,7168,256]{2,1,0:T(8,128)(2,1)} %param.23, bf16[32,1,7168]{2,0,1:T(8,128)(2,1)S(1)} %copy.43), kind=kOutput, calls=%fused_computation.22 | convolution fusion | flops 117440512 | bytes 4161536 | tf_op jit(solution)/shard_map/dot_general | solution.py:15
  199.6 5.3 %convolution_multiply_fusion.2 = f32[32,7168]{1,0:T(8,128)S(1)} fusion(bf16[3,256,7168]{2,1,0:T(8,128)(2,1)} %param.25, bf16[3,7168,256]{2,1,0:T(8,128)(2,1)} %param.24, bf16[32,1,7168]{2,0,1:T(8,128)(2,1)S(1)} %copy.43, f32[32]{0:T(128)S(1)} %get-tuple-element.8, f32[32,256]{1,0:T(8,128)S(1)} %fusion.18), kind=kOutput, calls=%fused_computation.4 | convolution fusion | flops 235159552 | bytes 8749184 | tf_op jit(solution)/shard_map/dot_general | solution.py:18
  204.9 5.3 %fusion.1 = f32[32,7168]{1,0:T(8,128)S(1)} fusion(f32[32,7168]{1,0:T(8,128)S(1)} %convolution_multiply_fusion.2, bf16[3,256,7168]{2,1,0:T(8,128)(2,1)} %param.25, bf16[3,7168,256]{2,1,0:T(8,128)(2,1)} %param.24, bf16[32,1,7168]{2,0,1:T(8,128)(2,1)S(1)} %copy.43, f32[32]{0:T(128)S(1)} %get-tuple-element.7, f32[32,256]{1,0:T(8,128)S(1)} %fusion.13), kind=kOutput, calls=%fused_computation.3 | convolution fusion | flops 235388928 | bytes 9666688 | tf_op jit(solution)/shard_map/dot_general | solution.py:18
  210.2 5.3 %fusion.3 = bf16[32,1,7168]{2,0,1:T(8,128)(2,1)S(1)} fusion(f32[32,7168]{1,0:T(8,128)S(1)} %fusion.1, bf16[3,256,7168]{2,1,0:T(8,128)(2,1)} %param.25, bf16[3,7168,256]{2,1,0:T(8,128)(2,1)} %param.24, bf16[32,1,7168]{2,0,1:T(8,128)(2,1)S(1)} %copy.43, f32[32]{0:T(128)S(1)} %get-tuple-element.6, f32[32,256]{1,0:T(8,128)S(1)} %fusion.8), kind=kOutput, calls=%fused_computation.6 | convolution fusion | flops 235618304 | bytes 9207936 | tf_op jit(solution)/shard_map/dot_general | solution.py:18
  215.4 0.9 reduce.15
  216.3 0.3 reshape.369
  216.6 17.0 %all_to_all.27 = bf16[32,2,3584]{2,1,0:T(2,128)(2,1)S(1)} all-to-all(bf16[32,2,3584]{2,1,0:T(2,128)(2,1)S(1)} %reshape.369), channel_id=1, replica_groups=mesh['group'=8,'local'=4] {'group','local'}, dimensions={0} | all-to-all | bytes 917504 | tf_op jit(solution)/shard_map/all_to_all | solution.py:125
  233.7 0.4 reshape.370
  234.0 2.9 %reduce.11 = bf16[32,7168]{1,0:T(8,128)(2,1)S(1)} reduce(bf16[32,1,7168]{2,1,0:T(2,128)(2,1)S(1)} %reshape.370, bf16[]{:T(256)} %constant.68), dimensions={1}, to_apply=%all_to_all.22.reduce_sub_computation | reduce | bytes 917506 | tf_op jit(solution)/shard_map/all_to_all | solution.py:125
  236.9 0.2 reshape.350
  237.1 0.6 reduce.9
  237.7 0.8 fusion.4
  (26 shorter events, 0.5 us)
Async XLA Ops:
  7.2 25.6 %copy-start = (bf16[4,512,128]{2,1,0:T(8,128)(2,1)S(1)}, bf16[4,512,128]{2,1,0:T(8,128)(2,1)}, u32[]{:S(2)}) copy-start(bf16[4,512,128]{2,1,0:T(8,128)(2,1)} %param.18) | copy-start | bytes 1572868
  7.2 16.5 %copy-start.4 = (f32[1,8]{1,0:T(1,128)S(1)}, f32[1,8]{1,0:T(1,128)}, u32[]{:S(2)}) copy-start(f32[1,8]{1,0:T(1,128)} %param.22) | copy-start | bytes 100
  7.2 17.7 %copy-start.5 = (s32[1,8]{1,0:T(1,128)S(1)}, s32[1,8]{1,0:T(1,128)}, u32[]{:S(2)}) copy-start(s32[1,8]{1,0:T(1,128)} %param.21) | copy-start | bytes 100
  16.3 15.5 %all-to-all-start = ((bf16[32,2,1024]{2,1,0:T(2,128)(2,1)}), bf16[32,2,1024]{2,1,0:T(2,128)(2,1)S(1)}, u32[]{:S(2)}, u32[]{:S(2)}) async-start(bf16[32,2,1024]{2,1,0:T(2,128)(2,1)} %reshape.365), calls=%async_computation | async-start | bytes 262144 | tf_op jit(solution)/shard_map/all_to_all | solution.py:65
  23.6 141.7 %all-reduce.3.cloned.1.call-start = ((), (), s32[]{:S(2)}) async-start(), calls=%async_computation.4 | async-start | bytes 1835008
  25.0 140.3 %copy-start.2 = (bf16[1,7168]{1,0:T(2,128)(2,1)S(1)}, bf16[1,7168]{1,0:T(2,128)(2,1)}, u32[]{:S(2)}) copy-start(bf16[1,7168]{1,0:T(2,128)(2,1)} %param.13) | copy-start | bytes 43012
  25.1 142.5 %copy-start.3 = (f32[7168]{0:T(1024)S(1)}, f32[7168]{0:T(1024)}, u32[]{:S(2)}) copy-start(f32[7168]{0:T(1024)} %param.20) | copy-start | bytes 86020
  39.7 133.2 %all-to-all-start.1 = ((bf16[32,1,3]{2,1,0:T(2,128)(2,1)}), bf16[32,1,3]{2,1,0:T(2,128)(2,1)S(1)}, u32[]{:S(2)}, u32[]{:S(2)}) async-start(bf16[32,1,3]{2,1,0:T(2,128)(2,1)} %copy.38), calls=%async_computation.1 | async-start | bytes 32768 | tf_op jit(solution)/shard_map/all_to_all | solution.py:116
  166.9 70.7 %copy-start.1 = (bf16[1,7168]{1,0:T(2,128)(2,1)}, bf16[1,7168]{1,0:T(2,128)(2,1)S(1)}, u32[]{:S(2)}) copy-start(bf16[1,7168]{1,0:T(2,128)(2,1)S(1)} %get-tuple-element.3) | copy-start | bytes 43012
  172.8 17.9 %all-to-all-start.2 = ((bf16[32,2,3584]{2,1,0:T(2,128)(2,1)}), bf16[32,2,3584]{2,1,0:T(2,128)(2,1)S(1)}, u32[]{:S(2)}, u32[]{:S(2)}) async-start(bf16[32,2,3584]{2,1,0:T(2,128)(2,1)} %reshape.367), calls=%async_computation.2 | async-start | bytes 917504 | tf_op jit(solution)/shard_map/all_to_all | solution.py:115
Sparse Core Ops, SparseCore 0:
  38.5 126.7 all-reduce.2
where the time goes:
time: 246 us; the launch traced here: 245 us
  waiting for transfers between devices  144 us (59%)
  matrix products  35.2 us (14%)
  blocking collectives  17 us (7%)
  between operations  15.6 us (6%)
  starting transfers between devices  13.6 us (6%)
  other arithmetic  13.3 us (5%)
  local copies, waits for them, and re-layouts  6.5 us (3%)
    unnamed x2, waiting for transfers between devices  123 us
    all_to_all x1, blocking collectives, body(): lax.all_to_all(partial_sums.reshape(group_count * local_count, requests,...  17 us
    dot_general x3, matrix products, expert_term(): output = jnp.dot(active, w_down[expert], preferred_element_type=jnp.float32)  15.8 us
    all_to_all x1, waiting for transfers between devices, body(): lax.all_to_all(copies, ('group', 'local'), split_axis=0, concat_axis=0, t...  14.1 us
    dot_general x3, matrix products, expert_term(): jnp.dot(slot_rows, w_gate[expert], preferred_element_type=jnp.float32)  8.33 us
    all_to_all x1, starting transfers between devices, body(): lax.all_to_all(latent_out, ('group', 'local'), split_axis=1, concat_axis=...  7.3 us
    all_to_all x1, waiting for transfers between devices, body(): lax.all_to_all(latent_out, ('group', 'local'), split_axis=1, concat_axis=...  6.78 us
    dot_general x1, matrix products, body(): jnp.dot(value_rows, w_out, preferred_element_type=jnp.float32)  5.45 us
  transfers between devices with their start and end apart: 4, of which 3 were waited for; matrix products, arithmetic and copies ran while one was open for 4% of the time, Pallas kernels for 0%

commit v1 on v0

v1 whole, which is shorter than its diff:
```python
import functools

import jax
import jax.numpy as jnp
from jax import lax
from jax.experimental import pallas as pl
from jax.experimental.pallas import tpu as pltpu
from jax.sharding import PartitionSpec as P

LAT = 512
ROPE = 64
VD = 128
CHUNKS = 2
SEG = 128
WIDE = 2
TILE = 16
MESH = pl.DeviceIdType.MESH
F32 = jnp.float32
BF16 = jnp.bfloat16


def kernel(
    dims,
    lengths,
    ids,
    scores,
    states,
    gain,
    kv_new,
    queries_hbm,
    cache_hbm,
    uv_hbm,
    out_hbm,
    gate_hbm,
    up_hbm,
    down_hbm,
    residual_out,
    layer_out,
    queries,
    cache,
    uv,
    wout,
    gate,
    up,
    down,
    lat32,
    lat_send,
    lat_got,
    stage,
    states32,
    gain32,
    res32,
    part,
    pair_got,
    pair_sum,
    row_got,
    rows,
    xmat,
    load_sem,
    lat_sem,
    pair_sem,
    scatter_sem,
    gather_sem,
    share_sem,
):
    group_count, local_count = dims
    n = group_count * local_count
    chips = n // 2
    group = lax.axis_index("group")
    local = lax.axis_index("local")
    me = group * local_count + local
    chip = me // 2
    core = lax.rem(me, 2)
    slot = core * chips + chip
    width = CHUNKS * SEG
    segs = states.shape[1] // width
    tall = stage.shape[0] // n
    heads = queries.shape[0]
    own_heads = uv.shape[0]
    per_head = lat32.shape[0] // heads
    lat_rows = own_heads * per_head
    experts, hidden = gate.shape[0], gate.shape[2]

    def device(index):
        return (index // local_count, lax.rem(index, local_count))

    partner = device(chip * 2 + 1 - core)

    first = [
        pltpu.make_async_copy(queries_hbm.at[0], queries, load_sem.at[0]),
        pltpu.make_async_copy(cache_hbm.at[0], cache, load_sem.at[1]),
    ]
    for copy in first:
        copy.start()
    barrier = pltpu.get_barrier_semaphore()

    def greet(k, carry):
        pl.semaphore_signal(
            barrier, inc=1, device_id=device(lax.rem(me + k, n)), device_id_type=MESH
        )
        return carry

    lax.fori_loop(1, n, greet, 0)

    load_uv = pltpu.make_async_copy(uv_hbm, uv, load_sem.at[2])
    load_out = pltpu.make_async_copy(out_hbm, wout, load_sem.at[3])
    load_gate = pltpu.make_async_copy(gate_hbm, gate, load_sem.at[4])
    load_up = pltpu.make_async_copy(up_hbm, up, load_sem.at[5])
    load_down = [
        pltpu.make_async_copy(
            down_hbm.at[e], down.at[pl.ds(e * hidden, hidden)], load_sem.at[6 + e]
        )
        for e in range(experts)
    ]

    states32[...] = jnp.zeros_like(states32)
    gain32[...] = jnp.zeros_like(gain32)
    stage[...] = jnp.zeros_like(stage)
    lat32[...] = jnp.zeros_like(lat32)
    for c in range(CHUNKS):
        for s in range(segs):
            at = (c * segs + s) * SEG
            states32[c, s : s + 1, :] = states[0:1, at : at + SEG].astype(F32)
            gain32[c, s : s + 1, :] = gain[0:1, at : at + SEG]

    lane = lax.broadcasted_iota(jnp.int32, (1, SEG), 1)
    score_sum = scores[0, 0]
    for k in range(1, scores.shape[1]):
        score_sum = score_sum + scores[0, k]
    dense = jnp.zeros((1, SEG), F32)
    for k in range(scores.shape[1]):
        weight = (
            jnp.full((1, SEG), 2.5 * scores[0, k], F32) / jnp.full((1, SEG), score_sum, F32)
        ).astype(BF16).astype(F32)
        dense = dense + jnp.where(lane == ids[0, k], weight, 0.0)

    for copy in first:
        copy.wait()
    for copy in [load_uv, load_out, load_gate, load_up] + load_down:
        copy.start()

    scale = (VD + ROPE) ** (-0.5)
    new = kv_new[...].astype(F32)
    cached = (
        lax.dot_general(
            queries[...], cache[...], (((1,), (1,)), ((), ())), preferred_element_type=F32
        )
        * scale
    )
    own = jnp.sum(queries[...].astype(F32) * new, axis=1, keepdims=True) * scale
    visible = lax.broadcasted_iota(jnp.int32, cached.shape, 1) < lengths[0]
    cached = jnp.where(visible, cached, -1e30)
    highest = jnp.maximum(jnp.max(cached, axis=1, keepdims=True), own)
    exps = jnp.exp(cached - highest)
    own_exp = jnp.exp(own - highest)
    denominator = jnp.sum(exps, axis=1, keepdims=True) + own_exp
    probs = (exps / denominator).astype(BF16)
    prob_own = (own_exp / denominator).astype(BF16).astype(F32)
    latent = jnp.dot(probs, cache[:, :LAT], preferred_element_type=F32)
    latent = latent + prob_own * new[:, :LAT]
    for q in range(LAT // 128):
        lat32[pl.ds(q, heads, stride=per_head), :] = latent[:, q * 128 : (q + 1) * 128]
    lat_send[...] = lat32[...].astype(BF16).reshape(lat_send.shape)

    pl.semaphore_wait(barrier, n - 1)

    def send_latent(k, carry):
        to = lax.rem(me + k, n)
        pltpu.make_async_remote_copy(
            src_ref=lat_send.at[to],
            dst_ref=lat_got.at[slot],
            send_sem=lat_sem.at[0],
            recv_sem=lat_sem.at[1],
            device_id=device(to),
            device_id_type=MESH,
        ).start()
        return carry

    lax.fori_loop(1, n, send_latent, 0)
    lat_got[pl.ds(slot, 1)] = lat_send[pl.ds(me, 1)]
    load_uv.wait()
    others = lat_got.at[pl.ds(0, n - 1)]
    pltpu.make_async_copy(others, others, lat_sem.at[1]).wait()
    lat32[...] = lat_got[...].astype(F32).reshape(lat32.shape)
    values = []
    for h in range(own_heads):
        by_head = jnp.concatenate(
            [
                lat32[pl.ds(h * per_head + q, n, stride=lat_rows), :]
                for q in range(LAT // 128)
            ],
            axis=1,
        ).astype(BF16)
        values.append(jnp.dot(by_head, uv[h], preferred_element_type=F32).astype(BF16))
    values = jnp.concatenate(values, axis=1)

    def scatter_sums(left, weight, turn):
        shares = []
        for c in range(CHUNKS):
            for s in range(0, segs, WIDE):
                at = (c * segs + s) * SEG
                product = jnp.dot(
                    left, weight[:, at : at + WIDE * SEG], preferred_element_type=F32
                )
                for w in range(WIDE):
                    stage[pl.ds(s + w, n, stride=tall), :] = product[:, w * SEG : (w + 1) * SEG]
            part[turn, c] = stage[...].astype(BF16).reshape(part.shape[2:])
            share = pltpu.make_async_remote_copy(
                src_ref=part.at[turn, c, pl.ds((1 - core) * chips, chips)],
                dst_ref=pair_got.at[turn, c],
                send_sem=pair_sem.at[0, turn, c],
                recv_sem=pair_sem.at[1, turn, c],
                device_id=partner,
                device_id_type=MESH,
            )
            share.start()
            shares.append(share)
        for c in range(CHUNKS):
            shares[c].wait()
            pair_sum[turn, c] = (
                part[turn, c, pl.ds(core * chips, chips)].astype(F32)
                + pair_got[turn, c].astype(F32)
            ).astype(BF16)

            def send_sum(k, carry):
                to = lax.rem(chip + k, chips)
                pltpu.make_async_remote_copy(
                    src_ref=pair_sum.at[turn, c, to],
                    dst_ref=row_got.at[turn, c, chip],
                    send_sem=scatter_sem.at[0, turn, c],
                    recv_sem=scatter_sem.at[1, turn, c],
                    device_id=device(to * 2 + core),
                    device_id_type=MESH,
                ).start()
                return carry

            lax.fori_loop(1, chips, send_sum, 0)
            row_got[turn, c, pl.ds(chip, 1)] = pair_sum[turn, c, pl.ds(chip, 1)]
        sums = []
        for c in range(CHUNKS):
            got = row_got.at[turn, c, pl.ds(0, chips - 1)]
            pltpu.make_async_copy(got, got, scatter_sem.at[1, turn, c]).wait()
            sums.append(jnp.sum(row_got[turn, c].astype(F32), axis=0))
        return sums

    load_out.wait()
    attention = scatter_sums(values, wout, 0)
    square = jnp.zeros((1, 1), F32)
    for c in range(CHUNKS):
        row = (states32[c] + attention[c]).astype(BF16).astype(F32)
        res32[c] = row
        square = square + jnp.sum(
            jnp.sum(row * row, axis=1, keepdims=True), axis=0, keepdims=True
        )
    factor = lax.rsqrt(square / states.shape[1] + 1e-6)
    for c in range(CHUNKS):
        normed = res32[c] * factor * gain32[c]
        if c == 0:
            at_row = lax.broadcasted_iota(jnp.int32, normed.shape, 0)
            normed = jnp.where(at_row == segs, dense, normed)
        rows[c, pl.ds(slot, 1)] = normed.astype(BF16)[None]

        def send_row(k, carry):
            to = lax.rem(chip + k, chips)
            pltpu.make_async_remote_copy(
                src_ref=rows.at[c, slot],
                dst_ref=rows.at[c, slot],
                send_sem=gather_sem.at[0, c],
                recv_sem=gather_sem.at[1, c],
                device_id=device(to * 2 + core),
                device_id_type=MESH,
            ).start()
            return carry

        lax.fori_loop(1, chips, send_row, 0)
    for c in range(CHUNKS):
        for s in range(segs):
            at = (c * segs + s) * SEG
            residual_out[0:1, at : at + SEG] = res32[c, s : s + 1, :].astype(BF16)
    shares = []
    for c in range(CHUNKS):
        got = rows.at[c, pl.ds(0, chips - 1)]
        pltpu.make_async_copy(got, got, gather_sem.at[1, c]).wait()
        mine = rows.at[c, pl.ds(core * chips, chips)]
        share = pltpu.make_async_remote_copy(
            src_ref=mine,
            dst_ref=mine,
            send_sem=share_sem.at[0, c],
            recv_sem=share_sem.at[1, c],
            device_id=partner,
            device_id_type=MESH,
        )
        share.start()
        shares.append(share)

    load_gate.wait()
    load_up.wait()
    gates = [None] * experts
    ups = [None] * experts
    weights = []
    deep = segs * SEG
    for c in range(CHUNKS):
        shares[c].wait()
        stage[...] = rows[c].astype(F32).reshape(stage.shape)
        for s in range(segs):
            xmat[:, s * SEG : (s + 1) * SEG] = stage[pl.ds(s, n, stride=tall), :].astype(BF16)
        if c == 0:
            table = stage[pl.ds(segs, n, stride=tall), :]
            lanes = lax.broadcasted_iota(jnp.int32, table.shape, 1)
            for e in range(experts):
                weights.append(
                    jnp.sum(
                        jnp.where(lanes == group * experts + e, table, 0.0),
                        axis=1,
                        keepdims=True,
                    )
                )
        left = xmat[...]
        for e in range(experts):
            gate_part = jnp.dot(
                left, gate[e, c * deep : (c + 1) * deep, :], preferred_element_type=F32
            )
            up_part = jnp.dot(
                left, up[e, c * deep : (c + 1) * deep, :], preferred_element_type=F32
            )
            gates[e] = gate_part if c == 0 else gates[e] + gate_part
            ups[e] = up_part if c == 0 else ups[e] + up_part
    active = jnp.concatenate(
        [
            (gates[e] / (1.0 + jnp.exp(-gates[e])) * ups[e] * weights[e]).astype(BF16)
            for e in range(experts)
        ],
        axis=1,
    )
    for copy in load_down:
        copy.wait()
    expert_sum = scatter_sums(active, down, 1)
    for c in range(CHUNKS):
        total = (res32[c] + expert_sum[c]).astype(BF16).astype(F32)
        res32[c] = total
        for s in range(segs):
            at = (c * segs + s) * SEG
            layer_out[0:1, at : at + SEG] = res32[c, s : s + 1, :].astype(BF16)

    sent = lat_send.at[pl.ds(0, n - 1)]
    pltpu.make_async_copy(sent, sent, lat_sem.at[0]).wait()
    for c in range(CHUNKS):
        sent = rows.at[c, pl.ds(0, chips - 1)]
        pltpu.make_async_copy(sent, sent, gather_sem.at[0, c]).wait()
        for turn in range(2):
            sent = pair_sum.at[turn, c, pl.ds(0, chips - 1)]
            pltpu.make_async_copy(sent, sent, scatter_sem.at[0, turn, c]).wait()


def body(
    group_count,
    local_count,
    states_in,
    queries,
    kv_cache,
    kv_new,
    lengths,
    w_uv,
    w_out,
    norm_gain,
    expert_ids,
    route_scores,
    w_gate,
    w_up,
    w_down,
):
    n = group_count * local_count
    chips = n // 2
    d = states_in.shape[1]
    heads, q_width = queries.shape[1:]
    cache_len = kv_cache.shape[1]
    own_heads = w_uv.shape[0]
    experts, _, hidden = w_gate.shape
    segs = d // (CHUNKS * SEG)
    tall = -(-(segs + 1) // TILE) * TILE
    per_head = max(LAT // 128, TILE // own_heads)
    lat_rows = own_heads * per_head
    smem = pl.BlockSpec(memory_space=pltpu.SMEM)
    vmem = pl.BlockSpec(memory_space=pltpu.VMEM)
    hbm = pl.BlockSpec(memory_space=pl.ANY)
    row = jax.ShapeDtypeStruct((1, d), BF16)
    return pl.pallas_call(
        functools.partial(kernel, (group_count, local_count)),
        out_shape=(row, row),
        in_specs=[smem] * 3 + [vmem] * 3 + [hbm] * 7,
        out_specs=(vmem, vmem),
        scratch_shapes=[
            pltpu.VMEM((heads, q_width), BF16),
            pltpu.VMEM((cache_len, q_width), BF16),
            pltpu.VMEM(w_uv.shape, BF16),
            pltpu.VMEM(w_out.shape, BF16),
            pltpu.VMEM(w_gate.shape, BF16),
            pltpu.VMEM(w_up.shape, BF16),
            pltpu.VMEM((experts * hidden, d), BF16),
            pltpu.VMEM((heads * per_head, 128), F32),
            pltpu.VMEM((n, lat_rows, 128), BF16),
            pltpu.VMEM((n, lat_rows, 128), BF16),
            pltpu.VMEM((n * tall, SEG), F32),
            pltpu.VMEM((CHUNKS, tall, SEG), F32),
            pltpu.VMEM((CHUNKS, tall, SEG), F32),
            pltpu.VMEM((CHUNKS, tall, SEG), F32),
            pltpu.VMEM((2, CHUNKS, n, tall, SEG), BF16),
            pltpu.VMEM((2, CHUNKS, chips, tall, SEG), BF16),
            pltpu.VMEM((2, CHUNKS, chips, tall, SEG), BF16),
            pltpu.VMEM((2, CHUNKS, chips, tall, SEG), BF16),
            pltpu.VMEM((CHUNKS, n, tall, SEG), BF16),
            pltpu.VMEM((n, segs * SEG), BF16),
            pltpu.SemaphoreType.DMA((6 + experts,)),
            pltpu.SemaphoreType.DMA((2,)),
            pltpu.SemaphoreType.DMA((2, 2, CHUNKS)),
            pltpu.SemaphoreType.DMA((2, 2, CHUNKS)),
            pltpu.SemaphoreType.DMA((2, CHUNKS)),
            pltpu.SemaphoreType.DMA((2, CHUNKS)),
        ],
        compiler_params=pltpu.CompilerParams(
            collective_id=0, has_side_effects=True, vmem_limit_bytes=60 * 1024 * 1024
        ),
    )(
        lengths,
        expert_ids,
        route_scores,
        states_in,
        norm_gain.reshape(1, d),
        kv_new,
        queries,
        kv_cache,
        w_uv,
        w_out,
        w_gate,
        w_up,
        w_down,
    )


def solution(mesh):
    in_specs = (
        P(("group", "local"), None),
        P(("group", "local"), None, None),
        P(("group", "local"), None, None),
        P(("group", "local"), None),
        P(("group", "local")),
        P(("group", "local"), None, None),
        P(("group", "local"), None),
        P(),
        P(("group", "local"), None),
        P(("group", "local"), None),
        P("group", None, "local"),
        P("group", None, "local"),
        P("group", "local", None),
    )
    out_specs = (P(("group", "local"), None), P(("group", "local"), None))
    sizes = (mesh.shape["group"], mesh.shape["local"])
    return jax.shard_map(
        functools.partial(body, *sizes),
        mesh=mesh,
        in_specs=in_specs,
        out_specs=out_specs,
        check_vma=False,
    )
```

time: 246 us -> 55.3 us (0.22)
  waiting for transfers between devices: 144 us -> 0 us
  Pallas kernels: 0 us -> 46.7 us
  matrix products: 35.2 us -> 0 us
  blocking collectives: 17 us -> 0 us
  between operations: 15.6 us -> 1.29 us
  starting transfers between devices: 13.6 us -> 0 us
  other arithmetic: 13.3 us -> 0 us
    unnamed x2 -> x0, waiting for transfers between devices: 123 us -> none
    pallas_call x0 -> x1, Pallas kernels: none -> 46.7 us  [body(): pl.pallas_call(functools.partial(kernel, (group_count, local_count)), out...]
    dot_general x12 -> x0, matrix products: 35.2 us -> none  [the longest x3 15.8 us: expert_term(): output = jnp.dot(active, w_down[expert], preferred_element_type=jnp.float32)]
    all_to_all x3 -> x0, waiting for transfers between devices: 20.9 us -> none  [the longest x1 14.1 us: body(): lax.all_to_all(copies, ('group', 'local'), split_axis=0, concat_axis=0, t...]
    all_to_all x1 -> x0, blocking collectives: 17 us -> none  [body(): lax.all_to_all(partial_sums.reshape(group_count * local_count, requests,...]
    all_to_all x3 -> x0, starting transfers between devices: 13.6 us -> none  [the longest x1 7.3 us: body(): lax.all_to_all(latent_out, ('group', 'local'), split_axis=1, concat_axis=...]
    broadcast_in_dim x1 -> x0, other arithmetic: 3.45 us -> none  [body(): jnp.broadcast_to(send_rows[:, None], (group_count, local_count) + send_ro...]
    unnamed x20 -> x4, local copies, waits for them, and re-layouts: 3.69 us -> 6.91 us
  transfers between devices with their start and end apart: 4 -> 0, of which waited for: 3 -> 0; matrix products, arithmetic and copies ran while one was open for 4% -> 0% of each run, Pallas kernels for 0% -> 0%
where the time goes in v1:
time: 55.3 us; the launch traced here: 54.9 us
  Pallas kernels  46.7 us (84%)
  local copies, waits for them, and re-layouts  6.91 us (12%)
  between operations  1.29 us (2%)
    pallas_call x1, Pallas kernels, body(): pl.pallas_call(functools.partial(kernel, (group_count, local_count)), out...  46.7 us
    unnamed x4, local copies, waits for them, and re-layouts  6.91 us

profile of v1, /device:TPU:0, one launch (start us, length us, event | category | flops | bytes accessed | tf_op | source)
XLA Modules:
  0.0 54.9 jit_solution(12129010961612034795)
XLA Ops:
  1.3 1.7 %copy.15.queries_hbm = bf16[1,128,576]{2,1,0:T(8,128)(2,1)} copy(bf16[1,128,576]{1,2,0:T(8,128)(2,1)} %param.14) | data formatting | bytes 294912 | tf_op args[1]
  3.0 2.4 %copy.16.cache_hbm = bf16[1,1024,576]{2,1,0:T(8,128)(2,1)} copy(bf16[1,1024,576]{1,2,0:T(8,128)(2,1)} %param.15) | data formatting | bytes 2359296 | tf_op args[2]
  5.4 46.7 %shard_map.140 = (bf16[1,7168]{1,0:T(2,128)(2,1)}, bf16[1,7168]{1,0:T(2,128)(2,1)}) custom-call(s32[1]{0:T(128)S(6)} %copy.19.lengths, s32[1,8]{1,0:T(1,128)} %ids.1, f32[1,8]{1,0:T(1,128)} %scores.1, bf16[1,7168]{1,0:T(2,128)(2,1)} %states.1, f32[1,7168]{1,0:T(1,128)} %bitcast.1, bf16[1,576]{1,0:T(2,128)(2,1)} %kv_new.1, ...), custom_call_target="tpu_custom_call" | custom-call | tf_op jit(solution)/shard_map/pallas_call | solution.py:387
  52.1 1.4 %copy.20 = bf16[1,7168]{1,0:T(2,128)(2,1)} copy(bf16[1,7168]{1,0:T(2,128)(2,1)} %get-tuple-element.4) | data formatting | bytes 28672
  53.5 1.4 %copy.21 = bf16[1,7168]{1,0:T(2,128)(2,1)} copy(bf16[1,7168]{1,0:T(2,128)(2,1)} %get-tuple-element.5) | data formatting | bytes 28672

commit v2 on v1

--- a/solution.py
+++ b/solution.py
@@ -14,6 +14,7 @@
 SEG = 128
 WIDE = 2
 TILE = 16
+SLOW = 4
 MESH = pl.DeviceIdType.MESH
 F32 = jnp.float32
 BF16 = jnp.bfloat16
@@ -34,8 +35,7 @@
     gate_hbm,
     up_hbm,
     down_hbm,
-    residual_out,
-    layer_out,
+    final,
     queries,
     cache,
     uv,
@@ -53,14 +53,18 @@
     part,
     pair_got,
     pair_sum,
+    plane_got,
+    plane_sum,
     row_got,
     rows,
     xmat,
     load_sem,
     lat_sem,
     pair_sem,
+    plane_sem,
     scatter_sem,
     gather_sem,
+    spread_sem,
     share_sem,
 ):
     group_count, local_count = dims
@@ -71,11 +75,14 @@
     me = group * local_count + local
     chip = me // 2
     core = lax.rem(me, 2)
-    slot = core * chips + chip
+    planes = SLOW if group_count % SLOW == 0 else 1
+    plane = chips // planes
+    far, near = chip // plane, lax.rem(chip, plane)
+    slot = core * chips + near * planes + far
     width = CHUNKS * SEG
     segs = states.shape[1] // width
     tall = stage.shape[0] // n
-    heads = queries.shape[0]
+    heads = queries.shape[1]
     own_heads = uv.shape[0]
     per_head = lat32.shape[0] // heads
     lat_rows = own_heads * per_head
@@ -83,6 +90,9 @@
 
     def device(index):
         return (index // local_count, lax.rem(index, local_count))
+
+    def same_core(to_far, to_near):
+        return device((to_far * plane + to_near) * 2 + core)
 
     partner = device(chip * 2 + 1 - core)
 
@@ -143,20 +153,27 @@
     new = kv_new[...].astype(F32)
     cached = (
         lax.dot_general(
-            queries[...], cache[...], (((1,), (1,)), ((), ())), preferred_element_type=F32
+            queries[...], cache[...], (((0,), (0,)), ((), ())), preferred_element_type=F32
         )
         * scale
     )
-    own = jnp.sum(queries[...].astype(F32) * new, axis=1, keepdims=True) * scale
+    own = (
+        lax.dot_general(
+            queries[...], kv_new[...], (((0,), (1,)), ((), ())), preferred_element_type=F32
+        )
+        * scale
+    )
     visible = lax.broadcasted_iota(jnp.int32, cached.shape, 1) < lengths[0]
     cached = jnp.where(visible, cached, -1e30)
     highest = jnp.maximum(jnp.max(cached, axis=1, keepdims=True), own)
     exps = jnp.exp(cached - highest)
     own_exp = jnp.exp(own - highest)
     denominator = jnp.sum(exps, axis=1, keepdims=True) + own_exp
-    probs = (exps / denominator).astype(BF16)
+    probs = (exps * (1.0 / denominator)).astype(BF16)
     prob_own = (own_exp / denominator).astype(BF16).astype(F32)
-    latent = jnp.dot(probs, cache[:, :LAT], preferred_element_type=F32)
+    latent = lax.dot_general(
+        probs, cache[:LAT, :], (((1,), (1,)), ((), ())), preferred_element_type=F32
+    )
     latent = latent + prob_own * new[:, :LAT]
     for q in range(LAT // 128):
         lat32[pl.ds(q, heads, stride=per_head), :] = latent[:, q * 128 : (q + 1) * 128]
@@ -196,7 +213,8 @@
 
     def scatter_sums(left, weight, turn):
         shares = []
-        for c in range(CHUNKS):
+
+        def multiply(c):
             for s in range(0, segs, WIDE):
                 at = (c * segs + s) * SEG
                 product = jnp.dot(
@@ -215,31 +233,57 @@
             )
             share.start()
             shares.append(share)
-        for c in range(CHUNKS):
+
+        def add_pair(c):
             shares[c].wait()
             pair_sum[turn, c] = (
-                part[turn, c, pl.ds(core * chips, chips)].astype(F32)
-                + pair_got[turn, c].astype(F32)
-            ).astype(BF16)
-
-            def send_sum(k, carry):
-                to = lax.rem(chip + k, chips)
+                (
+                    part[turn, c, pl.ds(core * chips, chips)].astype(F32)
+                    + pair_got[turn, c].astype(F32)
+                )
+                .astype(BF16)
+                .reshape(pair_sum.shape[2:])
+            )
+            for k in range(1, plane):
+                to = lax.rem(near + k, plane)
                 pltpu.make_async_remote_copy(
                     src_ref=pair_sum.at[turn, c, to],
-                    dst_ref=row_got.at[turn, c, chip],
+                    dst_ref=plane_got.at[turn, c, near],
+                    send_sem=plane_sem.at[0, turn, c],
+                    recv_sem=plane_sem.at[1, turn, c],
+                    device_id=same_core(far, to),
+                    device_id_type=MESH,
+                ).start()
+            plane_got[turn, c, pl.ds(near, 1)] = pair_sum[turn, c, pl.ds(near, 1)]
+
+        def add_plane(c):
+            got = plane_got.at[turn, c, pl.ds(0, plane - 1)]
+            pltpu.make_async_copy(got, got, plane_sem.at[1, turn, c]).wait()
+            plane_sum[turn, c] = jnp.sum(plane_got[turn, c].astype(F32), axis=0).astype(BF16)
+            for k in range(1, planes):
+                to = lax.rem(far + k, planes)
+                pltpu.make_async_remote_copy(
+                    src_ref=plane_sum.at[turn, c, to],
+                    dst_ref=row_got.at[turn, c, far],
                     send_sem=scatter_sem.at[0, turn, c],
                     recv_sem=scatter_sem.at[1, turn, c],
-                    device_id=device(to * 2 + core),
+                    device_id=same_core(to, near),
                     device_id_type=MESH,
                 ).start()
-                return carry
-
-            lax.fori_loop(1, chips, send_sum, 0)
-            row_got[turn, c, pl.ds(chip, 1)] = pair_sum[turn, c, pl.ds(chip, 1)]
+            row_got[turn, c, pl.ds(far, 1)] = plane_sum[turn, c, pl.ds(far, 1)]
+
+        for c in range(CHUNKS + 2):
+            if c < CHUNKS:
+                multiply(c)
+            if 0 <= c - 1 < CHUNKS:
+                add_pair(c - 1)
+            if 0 <= c - 2:
+                add_plane(c - 2)
         sums = []
         for c in range(CHUNKS):
-            got = row_got.at[turn, c, pl.ds(0, chips - 1)]
-            pltpu.make_async_copy(got, got, scatter_sem.at[1, turn, c]).wait()
+            if planes > 1:
+                got = row_got.at[turn, c, pl.ds(0, planes - 1)]
+                pltpu.make_async_copy(got, got, scatter_sem.at[1, turn, c]).wait()
             sums.append(jnp.sum(row_got[turn, c].astype(F32), axis=0))
         return sums
 
@@ -260,27 +304,35 @@
             normed = jnp.where(at_row == segs, dense, normed)
         rows[c, pl.ds(slot, 1)] = normed.astype(BF16)[None]
 
-        def send_row(k, carry):
-            to = lax.rem(chip + k, chips)
+        for k in range(1, planes):
             pltpu.make_async_remote_copy(
                 src_ref=rows.at[c, slot],
                 dst_ref=rows.at[c, slot],
                 send_sem=gather_sem.at[0, c],
                 recv_sem=gather_sem.at[1, c],
-                device_id=device(to * 2 + core),
+                device_id=same_core(lax.rem(far + k, planes), near),
                 device_id_type=MESH,
             ).start()
-            return carry
-
-        lax.fori_loop(1, chips, send_row, 0)
-    for c in range(CHUNKS):
-        for s in range(segs):
-            at = (c * segs + s) * SEG
-            residual_out[0:1, at : at + SEG] = res32[c, s : s + 1, :].astype(BF16)
     shares = []
-    for c in range(CHUNKS):
-        got = rows.at[c, pl.ds(0, chips - 1)]
-        pltpu.make_async_copy(got, got, gather_sem.at[1, c]).wait()
+
+    def spread(c):
+        if planes > 1:
+            got = rows.at[c, pl.ds(0, planes - 1)]
+            pltpu.make_async_copy(got, got, gather_sem.at[1, c]).wait()
+        mine = rows.at[c, pl.ds(core * chips + near * planes, planes)]
+        for k in range(1, plane):
+            pltpu.make_async_remote_copy(
+                src_ref=mine,
+                dst_ref=mine,
+                send_sem=spread_sem.at[0, c],
+                recv_sem=spread_sem.at[1, c],
+                device_id=same_core(far, lax.rem(near + k, plane)),
+                device_id_type=MESH,
+            ).start()
+
+    def hand_over(c):
+        got = rows.at[c, pl.ds(0, chips - planes)]
+        pltpu.make_async_copy(got, got, spread_sem.at[1, c]).wait()
         mine = rows.at[c, pl.ds(core * chips, chips)]
         share = pltpu.make_async_remote_copy(
             src_ref=mine,
@@ -292,6 +344,11 @@
         )
         share.start()
         shares.append(share)
+
+    for c in range(CHUNKS):
+        spread(c)
+        final[0, c] = res32[c]
+    hand_over(0)
 
     load_gate.wait()
     load_up.wait()
@@ -317,6 +374,8 @@
                 )
         left = xmat[...]
         for e in range(experts):
+            if e == 1 and c + 1 < CHUNKS:
+                hand_over(c + 1)
             gate_part = jnp.dot(
                 left, gate[e, c * deep : (c + 1) * deep, :], preferred_element_type=F32
             )
@@ -336,20 +395,31 @@
         copy.wait()
     expert_sum = scatter_sums(active, down, 1)
     for c in range(CHUNKS):
-        total = (res32[c] + expert_sum[c]).astype(BF16).astype(F32)
-        res32[c] = total
-        for s in range(segs):
-            at = (c * segs + s) * SEG
-            layer_out[0:1, at : at + SEG] = res32[c, s : s + 1, :].astype(BF16)
+        final[1, c] = res32[c] + expert_sum[c]
 
     sent = lat_send.at[pl.ds(0, n - 1)]
     pltpu.make_async_copy(sent, sent, lat_sem.at[0]).wait()
     for c in range(CHUNKS):
-        sent = rows.at[c, pl.ds(0, chips - 1)]
-        pltpu.make_async_copy(sent, sent, gather_sem.at[0, c]).wait()
+        if planes > 1:
+            sent = rows.at[c, pl.ds(0, planes - 1)]
+            pltpu.make_async_copy(sent, sent, gather_sem.at[0, c]).wait()
+        sent = rows.at[c, pl.ds(0, chips - planes)]
+        pltpu.make_async_copy(sent, sent, spread_sem.at[0, c]).wait()
         for turn in range(2):
-            sent = pair_sum.at[turn, c, pl.ds(0, chips - 1)]
-            pltpu.make_async_copy(sent, sent, scatter_sem.at[0, turn, c]).wait()
+            sent = pair_sum.at[turn, c, pl.ds(0, plane - 1)]
+            pltpu.make_async_copy(sent, sent, plane_sem.at[0, turn, c]).wait()
+            if planes > 1:
+                sent = plane_sum.at[turn, c, pl.ds(0, planes - 1)]
+                pltpu.make_async_copy(sent, sent, scatter_sem.at[0, turn, c]).wait()
+
+
+def write_rows(final, residual_out, layer_out):
+    segs = residual_out.shape[1] // (CHUNKS * SEG)
+    for which, out in enumerate((residual_out, layer_out)):
+        for c in range(CHUNKS):
+            for s in range(segs):
+                at = (c * segs + s) * SEG
+                out[0:1, at : at + SEG] = final[which, c, s : s + 1, :].astype(BF16)
 
 
 def body(
@@ -374,6 +444,8 @@
     d = states_in.shape[1]
     heads, q_width = queries.shape[1:]
     cache_len = kv_cache.shape[1]
+    planes = SLOW if group_count % SLOW == 0 else 1
+    plane = chips // planes
     own_heads = w_uv.shape[0]
     experts, _, hidden = w_gate.shape
     segs = d // (CHUNKS * SEG)
@@ -384,14 +456,14 @@
     vmem = pl.BlockSpec(memory_space=pltpu.VMEM)
     hbm = pl.BlockSpec(memory_space=pl.ANY)
     row = jax.ShapeDtypeStruct((1, d), BF16)
-    return pl.pallas_call(
+    final = pl.pallas_call(
         functools.partial(kernel, (group_count, local_count)),
-        out_shape=(row, row),
+        out_shape=jax.ShapeDtypeStruct((2, CHUNKS, tall, SEG), F32),
         in_specs=[smem] * 3 + [vmem] * 3 + [hbm] * 7,
-        out_specs=(vmem, vmem),
+        out_specs=vmem,
         scratch_shapes=[
-            pltpu.VMEM((heads, q_width), BF16),
-            pltpu.VMEM((cache_len, q_width), BF16),
+            pltpu.VMEM((q_width, heads), BF16),
+            pltpu.VMEM((q_width, cache_len), BF16),
             pltpu.VMEM(w_uv.shape, BF16),
             pltpu.VMEM(w_out.shape, BF16),
             pltpu.VMEM(w_gate.shape, BF16),
@@ -406,14 +478,18 @@
             pltpu.VMEM((CHUNKS, tall, SEG), F32),
             pltpu.VMEM((2, CHUNKS, n, tall, SEG), BF16),
             pltpu.VMEM((2, CHUNKS, chips, tall, SEG), BF16),
-            pltpu.VMEM((2, CHUNKS, chips, tall, SEG), BF16),
-            pltpu.VMEM((2, CHUNKS, chips, tall, SEG), BF16),
+            pltpu.VMEM((2, CHUNKS, plane, planes, tall, SEG), BF16),
+            pltpu.VMEM((2, CHUNKS, plane, planes, tall, SEG), BF16),
+            pltpu.VMEM((2, CHUNKS, planes, tall, SEG), BF16),
+            pltpu.VMEM((2, CHUNKS, planes, tall, SEG), BF16),
             pltpu.VMEM((CHUNKS, n, tall, SEG), BF16),
             pltpu.VMEM((n, segs * SEG), BF16),
             pltpu.SemaphoreType.DMA((6 + experts,)),
             pltpu.SemaphoreType.DMA((2,)),
             pltpu.SemaphoreType.DMA((2, 2, CHUNKS)),
             pltpu.SemaphoreType.DMA((2, 2, CHUNKS)),
+            pltpu.SemaphoreType.DMA((2, 2, CHUNKS)),
+            pltpu.SemaphoreType.DMA((2, CHUNKS)),
             pltpu.SemaphoreType.DMA((2, CHUNKS)),
             pltpu.SemaphoreType.DMA((2, CHUNKS)),
         ],
@@ -427,14 +503,17 @@
         states_in,
         norm_gain.reshape(1, d),
         kv_new,
-        queries,
-        kv_cache,
+        jnp.swapaxes(queries, 1, 2),
+        jnp.swapaxes(kv_cache, 1, 2),
         w_uv,
         w_out,
         w_gate,
         w_up,
         w_down,
     )
+    return pl.pallas_call(
+        write_rows, out_shape=(row, row), in_specs=[vmem], out_specs=(vmem, vmem)
+    )(final)
 
 
 def solution(mesh):

time: 55.3 us -> 53.7 us (0.971)
  local copies, waits for them, and re-layouts: 6.91 us -> 0 us
  Pallas kernels: 46.7 us -> 52.1 us
    unnamed x4 -> x0, local copies, waits for them, and re-layouts: 6.91 us -> none
    pallas_call x1, Pallas kernels: 46.7 us -> 50.6 us  [body(): pl.pallas_call(functools.partial(kernel, (group_count, local_count)), out...]
    pallas_call x0 -> x1, Pallas kernels: none -> 1.52 us  [body(): pl.pallas_call(write_rows, out_shape=(row, row), in_specs=[vmem], out_spe...]
where the time goes in v2:
time: 53.7 us; the launch traced here: 53.4 us
  Pallas kernels  52.1 us (97%)
  between operations  1.29 us (2%)
    pallas_call x1, Pallas kernels, body(): pl.pallas_call(functools.partial(kernel, (group_count, local_count)), out...  50.6 us
    pallas_call x1, Pallas kernels, body(): pl.pallas_call(write_rows, out_shape=(row, row), in_specs=[vmem], out_spe...  1.52 us

profile of v2, /device:TPU:0, one launch (start us, length us, event | category | flops | bytes accessed | tf_op | source)
XLA Modules:
  0.0 53.4 jit_solution(16469200285787165480)
XLA Ops:
  1.3 50.6 %shard_map.140.final = f32[2,2,32,128]{3,2,1,0:T(8,128)} custom-call(s32[1]{0:T(128)S(6)} %copy.15.lengths, s32[1,8]{1,0:T(1,128)} %ids.1, f32[1,8]{1,0:T(1,128)} %scores.1, bf16[1,7168]{1,0:T(2,128)(2,1)} %states.1, f32[1,7168]{1,0:T(1,128)} %bitcast.5, bf16[1,576]{1,0:T(2,128)(2,1)} %kv_new.1, bf16[1,576,128]{2,1,0:T(8,128)(2,1)} %bitcast.4, ...), custom_call_target="tpu_custom_call" | custom-call | tf_op jit(solution)/shard_map/pallas_call | solution.py:459
  51.9 1.5 %shard_map.141 = (bf16[1,7168]{1,0:T(2,128)(2,1)}, bf16[1,7168]{1,0:T(2,128)(2,1)}) custom-call(f32[2,2,32,128]{3,2,1,0:T(8,128)} %shard_map.140.final), custom_call_target="tpu_custom_call" | custom-call | tf_op jit(solution)/shard_map/pallas_call | solution.py:514

commit v3 on v2

--- a/solution.py
+++ b/solution.py
@@ -14,6 +14,7 @@
 SEG = 128
 WIDE = 2
 TILE = 16
+PIECES = 4
 SLOW = 4
 MESH = pl.DeviceIdType.MESH
 F32 = jnp.float32
@@ -113,15 +114,39 @@
     lax.fori_loop(1, n, greet, 0)
 
     load_uv = pltpu.make_async_copy(uv_hbm, uv, load_sem.at[2])
-    load_out = pltpu.make_async_copy(out_hbm, wout, load_sem.at[3])
-    load_gate = pltpu.make_async_copy(gate_hbm, gate, load_sem.at[4])
-    load_up = pltpu.make_async_copy(up_hbm, up, load_sem.at[5])
-    load_down = [
+    block = wout.shape[0] // PIECES
+    load_out = [
         pltpu.make_async_copy(
-            down_hbm.at[e], down.at[pl.ds(e * hidden, hidden)], load_sem.at[6 + e]
+            out_hbm.at[pl.ds(i * block, block)],
+            wout.at[pl.ds(i * block, block)],
+            load_sem.at[3 + i],
         )
-        for e in range(experts)
+        for i in range(PIECES)
     ]
+    deep = segs * SEG
+    load_gate = []
+    load_up = []
+    load_down = []
+    for c in range(CHUNKS):
+        for e in range(experts):
+            at = 3 + PIECES + (c * experts + e) * 3
+            half = pl.ds(c * deep, deep)
+            load_gate.append(
+                pltpu.make_async_copy(
+                    gate_hbm.at[e, half], gate.at[e, half], load_sem.at[at]
+                )
+            )
+            load_up.append(
+                pltpu.make_async_copy(up_hbm.at[e, half], up.at[e, half], load_sem.at[at + 1])
+            )
+            half_rows = hidden // CHUNKS
+            load_down.append(
+                pltpu.make_async_copy(
+                    down_hbm.at[e, pl.ds(c * half_rows, half_rows)],
+                    down.at[pl.ds(e * hidden + c * half_rows, half_rows)],
+                    load_sem.at[at + 2],
+                )
+            )
 
     states32[...] = jnp.zeros_like(states32)
     gain32[...] = jnp.zeros_like(gain32)
@@ -146,7 +171,7 @@
 
     for copy in first:
         copy.wait()
-    for copy in [load_uv, load_out, load_gate, load_up] + load_down:
+    for copy in [load_uv] + load_out:
         copy.start()
 
     scale = (VD + ROPE) ** (-0.5)
@@ -171,9 +196,12 @@
     denominator = jnp.sum(exps, axis=1, keepdims=True) + own_exp
     probs = (exps * (1.0 / denominator)).astype(BF16)
     prob_own = (own_exp / denominator).astype(BF16).astype(F32)
+    for i in range(len(load_gate)):
+        load_gate[i].start()
+        load_up[i].start()
     latent = lax.dot_general(
-        probs, cache[:LAT, :], (((1,), (1,)), ((), ())), preferred_element_type=F32
-    )
+        cache[:LAT, :], probs, (((1,), (1,)), ((), ())), preferred_element_type=F32
+    ).T
     latent = latent + prob_own * new[:, :LAT]
     for q in range(LAT // 128):
         lat32[pl.ds(q, heads, stride=per_head), :] = latent[:, q * 128 : (q + 1) * 128]
@@ -195,6 +223,8 @@
 
     lax.fori_loop(1, n, send_latent, 0)
     lat_got[pl.ds(slot, 1)] = lat_send[pl.ds(me, 1)]
+    for copy in load_down:
+        copy.start()
     load_uv.wait()
     others = lat_got.at[pl.ds(0, n - 1)]
     pltpu.make_async_copy(others, others, lat_sem.at[1]).wait()
@@ -287,7 +317,8 @@
             sums.append(jnp.sum(row_got[turn, c].astype(F32), axis=0))
         return sums
 
-    load_out.wait()
+    for copy in load_out:
+        copy.wait()
     attention = scatter_sums(values, wout, 0)
     square = jnp.zeros((1, 1), F32)
     for c in range(CHUNKS):
@@ -350,12 +381,9 @@
         final[0, c] = res32[c]
     hand_over(0)
 
-    load_gate.wait()
-    load_up.wait()
     gates = [None] * experts
     ups = [None] * experts
     weights = []
-    deep = segs * SEG
     for c in range(CHUNKS):
         shares[c].wait()
         stage[...] = rows[c].astype(F32).reshape(stage.shape)
@@ -376,6 +404,8 @@
         for e in range(experts):
             if e == 1 and c + 1 < CHUNKS:
                 hand_over(c + 1)
+            load_gate[c * experts + e].wait()
+            load_up[c * experts + e].wait()
             gate_part = jnp.dot(
                 left, gate[e, c * deep : (c + 1) * deep, :], preferred_element_type=F32
             )
@@ -484,7 +514,7 @@
             pltpu.VMEM((2, CHUNKS, planes, tall, SEG), BF16),
             pltpu.VMEM((CHUNKS, n, tall, SEG), BF16),
             pltpu.VMEM((n, segs * SEG), BF16),
-            pltpu.SemaphoreType.DMA((6 + experts,)),
+            pltpu.SemaphoreType.DMA((3 + PIECES + 3 * CHUNKS * experts,)),
             pltpu.SemaphoreType.DMA((2,)),
             pltpu.SemaphoreType.DMA((2, 2, CHUNKS)),
             pltpu.SemaphoreType.DMA((2, 2, CHUNKS)),

time: 53.7 us -> 54.5 us (1.015)
  Pallas kernels: 52.1 us -> 52.9 us
    pallas_call x1, Pallas kernels: 50.6 us -> 51.4 us  [body(): pl.pallas_call(functools.partial(kernel, (group_count, local_count)), out...]
where the time goes in v3:
time: 54.5 us; the launch traced here: 54.2 us
  Pallas kernels  52.9 us (97%)
  between operations  1.29 us (2%)
    pallas_call x1, Pallas kernels, body(): pl.pallas_call(functools.partial(kernel, (group_count, local_count)), out...  51.4 us
    pallas_call x1, Pallas kernels, body(): pl.pallas_call(write_rows, out_shape=(row, row), in_specs=[vmem], out_spe...  1.52 us

profile of v3, /device:TPU:0, one launch (start us, length us, event | category | flops | bytes accessed | tf_op | source)
XLA Modules:
  0.0 54.2 jit_solution(12096618226440650265)
XLA Ops:
  1.3 51.4 %shard_map.140.final = f32[2,2,32,128]{3,2,1,0:T(8,128)} custom-call(s32[1]{0:T(128)S(6)} %copy.15.lengths, s32[1,8]{1,0:T(1,128)} %ids.1, f32[1,8]{1,0:T(1,128)} %scores.1, bf16[1,7168]{1,0:T(2,128)(2,1)} %states.1, f32[1,7168]{1,0:T(1,128)} %bitcast.5, bf16[1,576]{1,0:T(2,128)(2,1)} %kv_new.1, bf16[1,576,128]{2,1,0:T(8,128)(2,1)} %bitcast.4, ...), custom_call_target="tpu_custom_call" | custom-call | tf_op jit(solution)/shard_map/pallas_call | solution.py:489
  52.7 1.5 %shard_map.141 = (bf16[1,7168]{1,0:T(2,128)(2,1)}, bf16[1,7168]{1,0:T(2,128)(2,1)}) custom-call(f32[2,2,32,128]{3,2,1,0:T(8,128)} %shard_map.140.final), custom_call_target="tpu_custom_call" | custom-call | tf_op jit(solution)/shard_map/pallas_call | solution.py:544

commit v4 on v3

--- a/solution.py
+++ b/solution.py
@@ -15,7 +15,7 @@
 WIDE = 2
 TILE = 16
 PIECES = 4
-SLOW = 4
+SLOW = 1
 MESH = pl.DeviceIdType.MESH
 F32 = jnp.float32
 BF16 = jnp.bfloat16
@@ -24,11 +24,11 @@
 def kernel(
     dims,
     lengths,
-    ids,
-    scores,
-    states,
-    gain,
-    kv_new,
+    ids_hbm,
+    scores_hbm,
+    states_hbm,
+    gain_hbm,
+    new_hbm,
     queries_hbm,
     cache_hbm,
     uv_hbm,
@@ -37,6 +37,11 @@
     up_hbm,
     down_hbm,
     final,
+    ids,
+    scores,
+    states,
+    gain,
+    kv_new,
     queries,
     cache,
     uv,
@@ -59,6 +64,7 @@
     row_got,
     rows,
     xmat,
+    small_sem,
     load_sem,
     lat_sem,
     pair_sem,
@@ -101,7 +107,19 @@
         pltpu.make_async_copy(queries_hbm.at[0], queries, load_sem.at[0]),
         pltpu.make_async_copy(cache_hbm.at[0], cache, load_sem.at[1]),
     ]
-    for copy in first:
+    small = [
+        pltpu.make_async_copy(source, target, small_sem.at[i])
+        for i, (source, target) in enumerate(
+            (
+                (ids_hbm, ids),
+                (scores_hbm, scores),
+                (states_hbm, states),
+                (gain_hbm, gain),
+                (new_hbm, kv_new),
+            )
+        )
+    ]
+    for copy in first + small:
         copy.start()
     barrier = pltpu.get_barrier_semaphore()
 
@@ -152,6 +170,8 @@
     gain32[...] = jnp.zeros_like(gain32)
     stage[...] = jnp.zeros_like(stage)
     lat32[...] = jnp.zeros_like(lat32)
+    for copy in small:
+        copy.wait()
     for c in range(CHUNKS):
         for s in range(segs):
             at = (c * segs + s) * SEG
@@ -289,6 +309,8 @@
         def add_plane(c):
             got = plane_got.at[turn, c, pl.ds(0, plane - 1)]
             pltpu.make_async_copy(got, got, plane_sem.at[1, turn, c]).wait()
+            if planes == 1:
+                return
             plane_sum[turn, c] = jnp.sum(plane_got[turn, c].astype(F32), axis=0).astype(BF16)
             for k in range(1, planes):
                 to = lax.rem(far + k, planes)
@@ -311,9 +333,11 @@
                 add_plane(c - 2)
         sums = []
         for c in range(CHUNKS):
-            if planes > 1:
-                got = row_got.at[turn, c, pl.ds(0, planes - 1)]
-                pltpu.make_async_copy(got, got, scatter_sem.at[1, turn, c]).wait()
+            if planes == 1:
+                sums.append(jnp.sum(plane_got[turn, c].astype(F32), axis=0)[0])
+                continue
+            got = row_got.at[turn, c, pl.ds(0, planes - 1)]
+            pltpu.make_async_copy(got, got, scatter_sem.at[1, turn, c]).wait()
             sums.append(jnp.sum(row_got[turn, c].astype(F32), axis=0))
         return sums
 
@@ -489,9 +513,14 @@
     final = pl.pallas_call(
         functools.partial(kernel, (group_count, local_count)),
         out_shape=jax.ShapeDtypeStruct((2, CHUNKS, tall, SEG), F32),
-        in_specs=[smem] * 3 + [vmem] * 3 + [hbm] * 7,
+        in_specs=[smem] + [hbm] * 12,
         out_specs=vmem,
         scratch_shapes=[
+            pltpu.SMEM(expert_ids.shape, jnp.int32),
+            pltpu.SMEM(route_scores.shape, F32),
+            pltpu.VMEM((1, d), BF16),
+            pltpu.VMEM((1, d), F32),
+            pltpu.VMEM(kv_new.shape, BF16),
             pltpu.VMEM((q_width, heads), BF16),
             pltpu.VMEM((q_width, cache_len), BF16),
             pltpu.VMEM(w_uv.shape, BF16),
@@ -514,6 +543,7 @@
             pltpu.VMEM((2, CHUNKS, planes, tall, SEG), BF16),
             pltpu.VMEM((CHUNKS, n, tall, SEG), BF16),
             pltpu.VMEM((n, segs * SEG), BF16),
+            pltpu.SemaphoreType.DMA((5,)),
             pltpu.SemaphoreType.DMA((3 + PIECES + 3 * CHUNKS * experts,)),
             pltpu.SemaphoreType.DMA((2,)),
             pltpu.SemaphoreType.DMA((2, 2, CHUNKS)),

time: 54.5 us -> 50 us (0.917)
  Pallas kernels: 52.9 us -> 48.5 us
    pallas_call x1, Pallas kernels: 51.4 us -> 47 us  [body(): pl.pallas_call(functools.partial(kernel, (group_count, local_count)), out...]
where the time goes in v4:
time: 50 us; the launch traced here: 49.8 us
  Pallas kernels  48.5 us (97%)
  between operations  1.29 us (3%)
    pallas_call x1, Pallas kernels, body(): pl.pallas_call(functools.partial(kernel, (group_count, local_count)), out...  47 us
    pallas_call x1, Pallas kernels, body(): pl.pallas_call(write_rows, out_shape=(row, row), in_specs=[vmem], out_spe...  1.52 us

profile of v4, /device:TPU:0, one launch (start us, length us, event | category | flops | bytes accessed | tf_op | source)
XLA Modules:
  0.0 49.8 jit_solution(15925711520836630868)
XLA Ops:
  1.3 47.0 %shard_map.140.final = f32[2,2,32,128]{3,2,1,0:T(8,128)} custom-call(s32[1]{0:T(128)S(6)} %copy.15.lengths, s32[1,8]{1,0:T(1,128)} %ids_hbm.1, f32[1,8]{1,0:T(1,128)} %scores_hbm.1, bf16[1,7168]{1,0:T(2,128)(2,1)} %states_hbm.1, f32[1,7168]{1,0:T(1,128)} %bitcast.5, bf16[1,576]{1,0:T(2,128)(2,1)} %new_hbm.1, bf16[1,576,128]{2,1,0:T(8,128)(2,1)} %bitcast.4, ...), custom_call_target="tpu_custom_call" | custom-call | tf_op jit(solution)/shard_map/pallas_call | solution.py:513
  48.3 1.5 %shard_map.141 = (bf16[1,7168]{1,0:T(2,128)(2,1)}, bf16[1,7168]{1,0:T(2,128)(2,1)}) custom-call(f32[2,2,32,128]{3,2,1,0:T(8,128)} %shard_map.140.final), custom_call_target="tpu_custom_call" | custom-call | tf_op jit(solution)/shard_map/pallas_call | solution.py:574

commit v5 on v4

--- a/solution.py
+++ b/solution.py
@@ -19,6 +19,10 @@
 MESH = pl.DeviceIdType.MESH
 F32 = jnp.float32
 BF16 = jnp.bfloat16
+
+
+def far_first(count):
+    return sorted(range(1, count), key=lambda k: abs(k - count // 2))
 
 
 def kernel(
@@ -216,9 +220,6 @@
     denominator = jnp.sum(exps, axis=1, keepdims=True) + own_exp
     probs = (exps * (1.0 / denominator)).astype(BF16)
     prob_own = (own_exp / denominator).astype(BF16).astype(F32)
-    for i in range(len(load_gate)):
-        load_gate[i].start()
-        load_up[i].start()
     latent = lax.dot_general(
         cache[:LAT, :], probs, (((1,), (1,)), ((), ())), preferred_element_type=F32
     ).T
@@ -230,7 +231,7 @@
     pl.semaphore_wait(barrier, n - 1)
 
     def send_latent(k, carry):
-        to = lax.rem(me + k, n)
+        to = lax.rem(me + n // 2 + (1 - 2 * lax.rem(k, 2)) * ((k + 1) // 2), n)
         pltpu.make_async_remote_copy(
             src_ref=lat_send.at[to],
             dst_ref=lat_got.at[slot],
@@ -241,8 +242,11 @@
         ).start()
         return carry
 
-    lax.fori_loop(1, n, send_latent, 0)
+    lax.fori_loop(0, n - 1, send_latent, 0)
     lat_got[pl.ds(slot, 1)] = lat_send[pl.ds(me, 1)]
+    for i in range(len(load_gate)):
+        load_gate[i].start()
+        load_up[i].start()
     for copy in load_down:
         copy.start()
     load_uv.wait()
@@ -294,7 +298,7 @@
                 .astype(BF16)
                 .reshape(pair_sum.shape[2:])
             )
-            for k in range(1, plane):
+            for k in far_first(plane):
                 to = lax.rem(near + k, plane)
                 pltpu.make_async_remote_copy(
                     src_ref=pair_sum.at[turn, c, to],
@@ -312,7 +316,7 @@
             if planes == 1:
                 return
             plane_sum[turn, c] = jnp.sum(plane_got[turn, c].astype(F32), axis=0).astype(BF16)
-            for k in range(1, planes):
+            for k in far_first(planes):
                 to = lax.rem(far + k, planes)
                 pltpu.make_async_remote_copy(
                     src_ref=plane_sum.at[turn, c, to],
@@ -359,7 +363,7 @@
             normed = jnp.where(at_row == segs, dense, normed)
         rows[c, pl.ds(slot, 1)] = normed.astype(BF16)[None]
 
-        for k in range(1, planes):
+        for k in far_first(planes):
             pltpu.make_async_remote_copy(
                 src_ref=rows.at[c, slot],
                 dst_ref=rows.at[c, slot],
@@ -375,7 +379,7 @@
             got = rows.at[c, pl.ds(0, planes - 1)]
             pltpu.make_async_copy(got, got, gather_sem.at[1, c]).wait()
         mine = rows.at[c, pl.ds(core * chips + near * planes, planes)]
-        for k in range(1, plane):
+        for k in far_first(plane):
             pltpu.make_async_remote_copy(
                 src_ref=mine,
                 dst_ref=mine,

time: 50 us -> 51.8 us (1.036)
  Pallas kernels: 48.5 us -> 50.3 us
    pallas_call x1, Pallas kernels: 47 us -> 48.8 us  [body(): pl.pallas_call(functools.partial(kernel, (group_count, local_count)), out...]
where the time goes in v5:
time: 51.8 us; the launch traced here: 51.6 us
  Pallas kernels  50.3 us (97%)
  between operations  1.29 us (2%)
    pallas_call x1, Pallas kernels, body(): pl.pallas_call(functools.partial(kernel, (group_count, local_count)), out...  48.8 us
    pallas_call x1, Pallas kernels, body(): pl.pallas_call(write_rows, out_shape=(row, row), in_specs=[vmem], out_spe...  1.52 us

profile of v5, /device:TPU:0, one launch (start us, length us, event | category | flops | bytes accessed | tf_op | source)
XLA Modules:
  0.0 51.6 jit_solution(14120834830160412192)
XLA Ops:
  1.3 48.8 %shard_map.140.final = f32[2,2,32,128]{3,2,1,0:T(8,128)} custom-call(s32[1]{0:T(128)S(6)} %copy.15.lengths, s32[1,8]{1,0:T(1,128)} %ids_hbm.1, f32[1,8]{1,0:T(1,128)} %scores_hbm.1, bf16[1,7168]{1,0:T(2,128)(2,1)} %states_hbm.1, f32[1,7168]{1,0:T(1,128)} %bitcast.5, bf16[1,576]{1,0:T(2,128)(2,1)} %new_hbm.1, bf16[1,576,128]{2,1,0:T(8,128)(2,1)} %bitcast.4, ...), custom_call_target="tpu_custom_call" | custom-call | tf_op jit(solution)/shard_map/pallas_call | solution.py:517
  50.0 1.5 %shard_map.141 = (bf16[1,7168]{1,0:T(2,128)(2,1)}, bf16[1,7168]{1,0:T(2,128)(2,1)}) custom-call(f32[2,2,32,128]{3,2,1,0:T(8,128)} %shard_map.140.final), custom_call_target="tpu_custom_call" | custom-call | tf_op jit(solution)/shard_map/pallas_call | solution.py:578
